TPU v7x, 512 devices: a whole 4x4x16 slice. The times are simulated.
512 devices in a mesh: layer: 4 (over y), row: 8 (over z_hi, x), col: 16 (over z_lo, core).
Axes of the slice: x: 4, y: 4, z: 16 (z_hi: 2, z_lo: 8; z = z_hi * 8 + z_lo), core: 2. Of those that a mesh axis runs over, the one named last changes fastest.
Arguments:
- pattern: int32 [1024, 8], replicated, may hold values from 0 to 1023, as said below
- density: float32 [1024, 8, 128, 128], P(('row', 'col'), 'layer'), may hold values from -2.5 to 2.5
Outputs:
- square: float32 [1024, 8, 128, 128], P(('row', 'col'), 'layer')
Inputs may be any that keep to these rules, and one draw needn't show every extreme that they name: `pattern`: each block row r lists 8 distinct block columns, all within 8 of r, its own column r among them.
All inputs are finite; a program needn't handle non-finite values.
Results may differ from a plain program's by a relative error of at most 0.0003.
Values sent between devices are 32-bit elements; how exact they have to be, the bound alone decides.
A program may use at most 128 MiB of HBM per device.

v0:
```python
import jax
import jax.numpy as jnp
from jax import lax
from jax.sharding import PartitionSpec as P


def padded(block, sides, width):
    for axis, dim in sides:
        count = lax.axis_size(axis)
        forward = [(i, i + 1) for i in range(count - 1)]
        backward = [(target, source) for source, target in forward]
        low = lax.ppermute(
            lax.slice_in_dim(block, block.shape[dim] - width, None, axis=dim), axis, forward
        )
        high = lax.ppermute(lax.slice_in_dim(block, 0, width, axis=dim), axis, backward)
        block = jnp.concatenate([low, block, high], axis=dim)
    return block


def per_device(pattern, density):
    rows = density.shape[0]
    quarter = density.shape[1]
    first = lax.axis_index(("row", "col")) * rows
    own_rows = lax.all_gather(density, "layer", axis=1, tiled=True)
    nearby = padded(own_rows, ((("row", "col"), 0),), rows)
    slot_start = lax.axis_index("layer") * quarter

    def term_row(local):
        columns = lax.dynamic_index_in_dim(pattern, first + local, 0, keepdims=False)
        mine = lax.dynamic_slice_in_dim(columns, slot_start, quarter, 0)
        blocks = lax.dynamic_index_in_dim(density, local, 0, keepdims=False)
        picked = jnp.take(nearby, mine - first + rows, axis=0)
        far_cols = jnp.take(pattern, mine, axis=0)
        match = (far_cols[:, :, None] == columns[None, None, :]).astype(jnp.float32)
        products = jnp.einsum("tij,tujk->tuik", blocks, picked, precision=lax.Precision.HIGHEST)
        return jnp.einsum("tus,tuik->sik", match, products, precision=lax.Precision.HIGHEST)

    partial_rows = lax.map(term_row, jnp.arange(rows, dtype=jnp.int32))
    return lax.psum_scatter(partial_rows, "layer", scatter_dimension=1, tiled=True)


def solution(mesh):
    in_specs = (P(), P(("row", "col"), "layer", None, None))
    out_specs = P(("row", "col"), "layer", None, None)
    return jax.shard_map(
        per_device, mesh=mesh, in_specs=in_specs, out_specs=out_specs, check_vma=False
    )
```

profile of v0, /device:TPU:6, one launch (start us, length us, event | category | flops | bytes accessed | tf_op | source)
XLA Modules:
  0.0 406.3 jit_solution(9060554406196078596)
XLA Ops:
  7.3 62.6 %all-gather.2.cloned.1.call-done = f32[8,8,128,128]{3,2,1,0:T(8,128)} async-done(((f32[8,2,128,128]{3,2,1,0:T(8,128)}), f32[8,8,128,128]{3,2,1,0:T(8,128)}) %all-gather.2.cloned.1.call-update) | async-done | bytes 4194320 | tf_op jit(solution)/shard_map/all_gather | solution.py:24
  69.9 1.9 collective-permute-start
  71.8 11.1 %collective-permute-start.1 = (f32[8,8,128,128]{3,2,1,0:T(8,128)}, f32[8,8,128,128]{3,2,1,0:T(8,128)}, u32[]{:S(2)}, u32[]{:S(2)}) collective-permute-start(f32[8,8,128,128]{3,2,1,0:T(8,128)} %all-gather.2.cloned.1.call-done), channel_id=1, source_target_pairs={{1,0},{2,1},{3,2},{4,3},{5,4},{6,5},{7,6},{8,7},{9,8},{10,9},{11,1... | collective-permute-start | bytes 12582920 | tf_op jit(solution)/shard_map/ppermute | solution.py:15
  83.0 1.0 copy.5
  83.9 84.7 %collective-permute-done = f32[8,8,128,128]{3,2,1,0:T(8,128)} collective-permute-done((f32[8,8,128,128]{3,2,1,0:T(8,128)}, f32[8,8,128,128]{3,2,1,0:T(8,128)}, u32[]{:S(2)}, u32[]{:S(2)}) %collective-permute-start) | collective-permute-done | bytes 4194336 | tf_op jit(solution)/shard_map/ppermute | solution.py:12
  168.7 9.5 %pad_maximum_fusion = f32[24,8,128,128]{3,2,1,0:T(8,128)} fusion(f32[8,8,128,128]{3,2,1,0:T(8,128)} %collective-permute-done.1, f32[8,8,128,128]{3,2,1,0:T(8,128)} %all-gather.2.cloned.1.call-done, f32[8,8,128,128]{3,2,1,0:T(8,128)} %collective-permute-done), kind=kLoop, calls=%fused_computation.32 | loop fusion | flops 6291456 | bytes 25165824 | tf_op jit(solution)/shard_map/concatenate | solution.py:16
  178.2 110.5 %while.13 = (s32[]{:T(128)}, f32[8,8,128,128]{3,2,1,0:T(8,128)}, s32[8]{0:T(128)S(1)}, s32[]{:T(128)}, s32[1024,8]{1,0:T(8,128)S(1)}, /*index=5*/s32[]{:T(128)},...) while((s32[]{:T(128)}, f32[8,8,128,128]{3,2,1,0:T(8,128)}, ...), condition=%wide.region_1.2_spmd, body=%wide.region_0.1_spmd.sunk | while | flops 428083392 | bytes 9053433 | solution.py:38
  179.5 5.2 %gather_fusion = f32[2,8,128,128]{3,2,1,0:T(8,128)S(1)} fusion(f32[24,8,128,128]{3,2,1,0:T(8,128)} %get-tuple-element.279, s32[1024]{0:T(1024)S(1)} %get-tuple-element.244), kind=kCustom, calls=%fused_computation.1.clone.1 | custom fusion | bytes 2097160 | tf_op jit(solution)/shard_map/while/body/eval_jaxpr/jit(_take)/gather | solution.py:32
  186.6 2.8 fusion.28
  191.1 0.9 copy_dynamic-update-slice_fusion.2
  193.3 5.2 %gather_fusion = f32[2,8,128,128]{3,2,1,0:T(8,128)S(1)} fusion(f32[24,8,128,128]{3,2,1,0:T(8,128)} %get-tuple-element.279, s32[1024]{0:T(1024)S(1)} %get-tuple-element.244), kind=kCustom, calls=%fused_computation.1.clone.1 | custom fusion | bytes 2097160 | tf_op jit(solution)/shard_map/while/body/eval_jaxpr/jit(_take)/gather | solution.py:32
  200.4 2.8 fusion.28
  204.9 0.9 copy_dynamic-update-slice_fusion.2
  207.1 5.2 %gather_fusion = f32[2,8,128,128]{3,2,1,0:T(8,128)S(1)} fusion(f32[24,8,128,128]{3,2,1,0:T(8,128)} %get-tuple-element.279, s32[1024]{0:T(1024)S(1)} %get-tuple-element.244), kind=kCustom, calls=%fused_computation.1.clone.1 | custom fusion | bytes 2097160 | tf_op jit(solution)/shard_map/while/body/eval_jaxpr/jit(_take)/gather | solution.py:32
  214.2 2.8 fusion.28
  218.7 0.9 copy_dynamic-update-slice_fusion.2
  220.9 5.2 %gather_fusion = f32[2,8,128,128]{3,2,1,0:T(8,128)S(1)} fusion(f32[24,8,128,128]{3,2,1,0:T(8,128)} %get-tuple-element.279, s32[1024]{0:T(1024)S(1)} %get-tuple-element.244), kind=kCustom, calls=%fused_computation.1.clone.1 | custom fusion | bytes 2097160 | tf_op jit(solution)/shard_map/while/body/eval_jaxpr/jit(_take)/gather | solution.py:32
  228.0 2.8 fusion.28
  234.7 5.2 %gather_fusion = f32[2,8,128,128]{3,2,1,0:T(8,128)S(1)} fusion(f32[24,8,128,128]{3,2,1,0:T(8,128)} %get-tuple-element.279, s32[1024]{0:T(1024)S(1)} %get-tuple-element.244), kind=kCustom, calls=%fused_computation.1.clone.1 | custom fusion | bytes 2097160 | tf_op jit(solution)/shard_map/while/body/eval_jaxpr/jit(_take)/gather | solution.py:32
  241.8 2.8 fusion.28
  246.3 0.9 copy_dynamic-update-slice_fusion.2
  248.5 5.2 %gather_fusion = f32[2,8,128,128]{3,2,1,0:T(8,128)S(1)} fusion(f32[24,8,128,128]{3,2,1,0:T(8,128)} %get-tuple-element.279, s32[1024]{0:T(1024)S(1)} %get-tuple-element.244), kind=kCustom, calls=%fused_computation.1.clone.1 | custom fusion | bytes 2097160 | tf_op jit(solution)/shard_map/while/body/eval_jaxpr/jit(_take)/gather | solution.py:32
  255.6 2.8 fusion.28
  262.3 5.2 %gather_fusion = f32[2,8,128,128]{3,2,1,0:T(8,128)S(1)} fusion(f32[24,8,128,128]{3,2,1,0:T(8,128)} %get-tuple-element.279, s32[1024]{0:T(1024)S(1)} %get-tuple-element.244), kind=kCustom, calls=%fused_computation.1.clone.1 | custom fusion | bytes 2097160 | tf_op jit(solution)/shard_map/while/body/eval_jaxpr/jit(_take)/gather | solution.py:32
  269.4 2.8 fusion.28
  273.9 0.9 copy_dynamic-update-slice_fusion.2
  276.2 5.2 %gather_fusion = f32[2,8,128,128]{3,2,1,0:T(8,128)S(1)} fusion(f32[24,8,128,128]{3,2,1,0:T(8,128)} %get-tuple-element.279, s32[1024]{0:T(1024)S(1)} %get-tuple-element.244), kind=kCustom, calls=%fused_computation.1.clone.1 | custom fusion | bytes 2097160 | tf_op jit(solution)/shard_map/while/body/eval_jaxpr/jit(_take)/gather | solution.py:32
  283.2 2.8 fusion.28
  287.7 0.9 copy_dynamic-update-slice_fusion.2
  288.7 1.3 dynamic-slice.5
  290.6 106.6 %all-reduce.3.cloned.1.call-done = f32[8,8,128,128]{3,2,1,0:T(8,128)} async-done(((f32[8,8,128,128]{3,2,1,0:T(8,128)}), f32[8,8,128,128]{3,2,1,0:T(8,128)}) %all-reduce.3.cloned.1.call-update) | async-done | bytes 4194320
  397.2 2.3 constant_dynamic-slice_fusion.1
  (89 shorter events, 21.7 us)
Async XLA Ops:
  6.5 63.3 %all-gather.2.cloned.1.call-start = ((), (), s32[]{:S(2)}) async-start(), calls=%async_computation | async-start | bytes 5242880 | tf_op jit(solution)/shard_map/all_gather | solution.py:24
  7.3 390.0 %all-reduce.3.cloned.1.call-start = ((), (), s32[]{:S(2)}) async-start(), calls=%async_computation.1 | async-start | bytes 8388608
  69.9 98.8 %collective-permute-start = (f32[8,8,128,128]{3,2,1,0:T(8,128)}, f32[8,8,128,128]{3,2,1,0:T(8,128)}, u32[]{:S(2)}, u32[]{:S(2)}) collective-permute-start(f32[8,8,128,128]{3,2,1,0:T(8,128)} %all-gather.2.cloned.1.call-done), channel_id=1, source_target_pairs={{0,1},{1,2},{2,3},{3,4},{4,5},{5,6},{6,7},{7,8},{8,9},{9,10},{10,1... | collective-permute-start | bytes 12582920 | tf_op jit(solution)/shard_map/ppermute | solution.py:12
  71.8 96.9 %collective-permute-start.1 = (f32[8,8,128,128]{3,2,1,0:T(8,128)}, f32[8,8,128,128]{3,2,1,0:T(8,128)}, u32[]{:S(2)}, u32[]{:S(2)}) collective-permute-start(f32[8,8,128,128]{3,2,1,0:T(8,128)} %all-gather.2.cloned.1.call-done), channel_id=1, source_target_pairs={{1,0},{2,1},{3,2},{4,3},{5,4},{6,5},{7,6},{8,7},{9,8},{10,9},{11,1... | collective-permute-start | bytes 12582920 | tf_op jit(solution)/shard_map/ppermute | solution.py:15
Sparse Core Ops, SparseCore 0:
  9.5 60.3 all-gather.1
  288.8 108.3 all-reduce.2
where the time goes:
time: 408 us; the launch traced here: 406 us
  waiting for transfers between devices  255 us (62%)
  local copies, waits for them, and re-layouts  66.6 us (16%)
  matrix products  26.6 us (7%)
  loops' own time  20.3 us (5%)
  between operations  14.1 us (3%)
  starting transfers between devices  13.1 us (3%)
  other arithmetic  10.9 us (3%)
    unnamed x3, waiting for transfers between devices  107 us
    ppermute x1, waiting for transfers between devices, padded(): lax.ppermute(lax.slice_in_dim(block, block.shape[dim] - width, None, axis...  84.7 us
    all_gather x1, waiting for transfers between devices, per_device(): own_rows = lax.all_gather(density, 'layer', axis=1, tiled=True)  62.6 us
    gather x8, local copies, waits for them, and re-layouts, term_row(): picked = jnp.take(nearby, mine - first + rows, axis=0)  41.5 us
    dot_general x8, matrix products, term_row(): jnp.einsum('tij,tujk->tuik', blocks, picked, precision=lax.Precision.HIGH...  22.2 us
    another operation x1, loops' own time, per_device(): partial_rows = lax.map(term_row, jnp.arange(rows, dtype=jnp.int32))  20.3 us
    ppermute x1, starting transfers between devices, padded(): lax.ppermute(lax.slice_in_dim(block, 0, width, axis=dim), axis, backward)  11.1 us
    concatenate x1, other arithmetic, padded(): block = jnp.concatenate([low, block, high], axis=dim)  9.48 us
  transfers between devices with their start and end apart: 4, of which 3 were waited for; matrix products, arithmetic and copies ran while one was open for 1% of the time, Pallas kernels for 0%

commit v1 on v0

v1 whole, which is shorter than its diff:
```python
import jax
import jax.numpy as jnp
from jax import lax
from jax.experimental import pallas as pl
from jax.experimental.pallas import tpu as pltpu
from jax.sharding import PartitionSpec as P

MESH = pl.DeviceIdType.MESH
LAYERS, ROWS_AXIS, COLS_AXIS, RUNS = 4, 8, 16, 4
ROWS, SLOTS, QUARTER, BS = 8, 8, 2, 128
BLOCKS = ROWS * QUARTER
GROUP = LAYERS * BLOCKS
CHUNKS = 4
CB = BLOCKS // CHUNKS


def kernel(
    pat_ref, den_ref, out_ref,
    near, part, pat, tab_near, tab_part, a_hi, a_lo, m_hi, m_lo, acc,
    near_sem, part_sem, send_sem, local_sem, pat_sem, out_sem,
):
    l, row, col = (lax.axis_index(a) for a in ("layer", "row", "col"))
    core = lax.rem(col, 2)
    g = row * COLS_AXIS + col
    up, dn, opp = lax.rem(l + 1, 4), lax.rem(l + 3, 4), lax.rem(l + 2, 4)
    pg = lax.rem(g + jnp.where(core == 0, 127, 1), 128)
    at_up, at_dn = (up, row, col), (dn, row, col)
    at_mate = (l, row, col + 1 - 2 * core)
    at_part = (l, lax.div(pg, COLS_AXIS), lax.rem(pg, COLS_AXIS))
    x = lax.rem(row, RUNS)
    far = jnp.logical_or(
        jnp.logical_and(col == 0, x != 0),
        jnp.logical_and(col == COLS_AXIS - 1, x != RUNS - 1),
    )
    close = jnp.logical_not(far)

    barrier = pltpu.get_barrier_semaphore()
    for peer in (at_up, at_dn, at_mate, at_part):
        pl.semaphore_signal(barrier, inc=1, device_id=peer, device_id_type=MESH)

    sent = []

    def send(src, dst, sem, peer, when=None):
        n = len(sent)
        copy = pltpu.make_async_remote_copy(
            src_ref=src, dst_ref=dst, send_sem=send_sem.at[n], recv_sem=sem,
            device_id=peer, device_id_type=MESH,
        )
        sent.append((copy, when))
        if when is None:
            copy.start()
        else:
            pl.when(when)(copy.start)

    def piece(ref, base, layer, j):
        return ref.at[pl.ds(base + layer * BLOCKS + j * CB, CB)]

    def own(layer, j):
        return piece(near, 0, layer, j)

    def mate(layer, j):
        return piece(near, GROUP, layer, j)

    def halo(layer, j):
        return piece(part, 0, layer, j)

    def own_sem(layer, j):
        return near_sem.at[layer * CHUNKS + j]

    def mate_sem(layer, j):
        return near_sem.at[LAYERS * CHUNKS + layer * CHUNKS + j]

    def halo_sem(layer, j):
        return part_sem.at[layer * CHUNKS + j]

    def arrived(ref, sem):
        pltpu.make_async_remote_copy(
            src_ref=ref, dst_ref=ref, send_sem=send_sem.at[0], recv_sem=sem,
            device_id=at_mate, device_id_type=MESH,
        ).wait_recv()

    pat_copies = []
    for k in range(3):
        kg = lax.rem(g + 127 + k, 128)
        c = pltpu.make_async_copy(
            pat_ref.at[pl.ds(pl.multiple_of(kg * ROWS, ROWS), ROWS)], pat.at[pl.ds(k * ROWS, ROWS)], pat_sem.at[k]
        )
        c.start()
        pat_copies.append(c)
    mine = pltpu.make_async_copy(den_ref, near.at[pl.ds(l * BLOCKS, BLOCKS)], local_sem)
    mine.start()
    pl.semaphore_wait(barrier, 4)

    for j in range(CHUNKS):
        src = den_ref.at[pl.ds(j * CB, CB)]
        send(src, halo(l, j), halo_sem(l, j), at_part)
        send(src, own(l, j), own_sem(l, j), at_up)
        send(src, own(l, j), own_sem(l, j), at_dn)
        send(src, mate(l, j), mate_sem(l, j), at_mate)

    near[2 * GROUP] = jnp.zeros((BS, BS), jnp.float32)
    part[GROUP] = jnp.zeros((BS, BS), jnp.float32)
    for c in pat_copies:
        c.wait()

    def index_row(r, carry):
        wanted = [pat[ROWS + r, 2 * l + s] for s in range(QUARTER)]
        for t in range(SLOTS):
            q = jnp.clip(pat[ROWS + r, t] - ROWS * (g - 1), 0, 3 * ROWS - 1)
            grp, qrow = lax.div(q, ROWS), lax.rem(q, ROWS)
            is_own = grp == 1
            is_mate = grp == 2 - 2 * core
            is_near = jnp.logical_or(is_own, is_mate)
            base = qrow * QUARTER
            at = [jnp.int32(-1)] * QUARTER
            for u in range(SLOTS):
                v = pat[q, u]
                for s in range(QUARTER):
                    at[s] = jnp.where(v == wanted[s], base + (u // 2) * BLOCKS + u % 2, at[s])
            for s in range(QUARTER):
                hit = at[s] >= 0
                tab_near[r * 16 + t * 2 + s] = jnp.where(
                    jnp.logical_and(hit, is_near), at[s] + jnp.where(is_own, 0, GROUP), 2 * GROUP
                )
                tab_part[r * 16 + t * 2 + s] = jnp.where(
                    jnp.logical_and(hit, jnp.logical_not(is_near)), at[s], GROUP
                )
        return carry

    lax.fori_loop(0, ROWS, index_row, 0)

    for j in range(CHUNKS):
        arrived(own(dn, j), own_sem(dn, j))
        if j < CHUNKS // 2:
            send(own(dn, j), own(dn, j), own_sem(dn, j), at_up)
        send(own(dn, j), halo(dn, j), halo_sem(dn, j), at_part, close)
        send(own(dn, j), mate(dn, j), mate_sem(dn, j), at_mate)
        arrived(own(up, j), own_sem(up, j))
        if j >= CHUNKS // 2:
            send(own(up, j), own(up, j), own_sem(up, j), at_dn)
        send(own(up, j), halo(up, j), halo_sem(up, j), at_part, close)
        send(own(up, j), mate(up, j), mate_sem(up, j), at_mate)
        arrived(halo(l, j), halo_sem(l, j))
        send(halo(l, j), halo(l, j), halo_sem(l, j), at_up, far)
        send(halo(l, j), halo(l, j), halo_sem(l, j), at_dn, far)
    for j in range(CHUNKS):
        arrived(own(opp, j), own_sem(opp, j))
        send(own(opp, j), mate(opp, j), mate_sem(opp, j), at_mate)
        arrived(halo(dn, j), halo_sem(dn, j))
        if j < CHUNKS // 2:
            send(halo(dn, j), halo(dn, j), halo_sem(dn, j), at_up)
        arrived(halo(up, j), halo_sem(up, j))
        if j >= CHUNKS // 2:
            send(halo(up, j), halo(up, j), halo_sem(up, j), at_dn)
    mine.wait()
    for layer in range(LAYERS):
        for j in range(CHUNKS):
            arrived(mate(layer, j), mate_sem(layer, j))

    def split(v):
        hi = v.astype(jnp.bfloat16)
        return hi, (v - hi.astype(jnp.float32)).astype(jnp.bfloat16)

    def product(r, ref, tab):
        for t in range(SLOTS):
            for s in range(QUARTER):
                hi, lo = split(ref[tab[r * 16 + t * 2 + s]])
                m_hi[t * BS:(t + 1) * BS, s * BS:(s + 1) * BS] = hi
                m_lo[t * BS:(t + 1) * BS, s * BS:(s + 1) * BS] = lo
        h, w = a_hi[r], m_hi[...]
        total = jnp.dot(h, w, preferred_element_type=jnp.float32)
        total += jnp.dot(h, m_lo[...], preferred_element_type=jnp.float32)
        return total + jnp.dot(a_lo[r], w, preferred_element_type=jnp.float32)

    def near_row(r, carry):
        for t in range(SLOTS):
            hi, lo = split(near[(t // 2) * BLOCKS + r * QUARTER + t % 2])
            a_hi[r, :, t * BS:(t + 1) * BS] = hi
            a_lo[r, :, t * BS:(t + 1) * BS] = lo
        total = product(r, near, tab_near)
        for s in range(QUARTER):
            acc[r * QUARTER + s] = total[:, s * BS:(s + 1) * BS]
        return carry

    lax.fori_loop(0, ROWS, near_row, 0)

    for j in range(CHUNKS):
        arrived(halo(opp, j), halo_sem(opp, j))

    def part_row(r, carry):
        total = product(r, part, tab_part)
        for s in range(QUARTER):
            acc[r * QUARTER + s] += total[:, s * BS:(s + 1) * BS]
        return carry

    lax.fori_loop(0, ROWS, part_row, 0)
    done = pltpu.make_async_copy(acc, out_ref, out_sem)
    done.start()
    for copy, when in sent:
        if when is None:
            copy.wait_send()
        else:
            pl.when(when)(copy.wait_send)
    done.wait()


def per_device(pattern, density):
    shape = density.shape
    flat = density.reshape(BLOCKS, BS, BS)
    f32, bf16 = jnp.float32, jnp.bfloat16
    result = pl.pallas_call(
        kernel,
        out_shape=jax.ShapeDtypeStruct((BLOCKS, BS, BS), f32),
        in_specs=[pl.BlockSpec(memory_space=pl.ANY)] * 2,
        out_specs=pl.BlockSpec(memory_space=pl.ANY),
        scratch_shapes=[
            pltpu.VMEM((2 * GROUP + 1, BS, BS), f32),
            pltpu.VMEM((GROUP + 1, BS, BS), f32),
            pltpu.SMEM((3 * ROWS, SLOTS), jnp.int32),
            pltpu.SMEM((ROWS * SLOTS * QUARTER,), jnp.int32),
            pltpu.SMEM((ROWS * SLOTS * QUARTER,), jnp.int32),
            pltpu.VMEM((ROWS, BS, SLOTS * BS), bf16),
            pltpu.VMEM((ROWS, BS, SLOTS * BS), bf16),
            pltpu.VMEM((SLOTS * BS, QUARTER * BS), bf16),
            pltpu.VMEM((SLOTS * BS, QUARTER * BS), bf16),
            pltpu.VMEM((BLOCKS, BS, BS), f32),
            pltpu.SemaphoreType.DMA((2 * LAYERS * CHUNKS,)),
            pltpu.SemaphoreType.DMA((LAYERS * CHUNKS,)),
            pltpu.SemaphoreType.DMA((13 * CHUNKS,)),
            pltpu.SemaphoreType.DMA,
            pltpu.SemaphoreType.DMA((3,)),
            pltpu.SemaphoreType.DMA,
        ],
        compiler_params=pltpu.CompilerParams(
            collective_id=0, has_side_effects=True, vmem_limit_bytes=40 * 1024 * 1024
        ),
        cost_estimate=pl.CostEstimate(flops=3 * 2**29, bytes_accessed=2**24, transcendentals=0),
    )(pattern, flat)
    return result.reshape(shape)


def solution(mesh):
    in_specs = (P(), P(("row", "col"), "layer", None, None))
    out_specs = P(("row", "col"), "layer", None, None)
    return jax.shard_map(
        per_device, mesh=mesh, in_specs=in_specs, out_specs=out_specs, check_vma=False
    )
```

time: 408 us -> 71.4 us (0.18)
  waiting for transfers between devices: 255 us -> 0 us
  Pallas kernels: 0 us -> 68 us
  local copies, waits for them, and re-layouts: 66.6 us -> 3.15 us
  matrix products: 26.6 us -> 0 us
  loops' own time: 20.3 us -> 0 us
  between operations: 14.1 us -> 0.03 us
  starting transfers between devices: 13.1 us -> 0 us
  other arithmetic: 10.9 us -> 0 us
    unnamed x3 -> x0, waiting for transfers between devices: 107 us -> none
    ppermute x2 -> x0, waiting for transfers between devices: 84.7 us -> none  [the longest x1 84.7 us: padded(): lax.ppermute(lax.slice_in_dim(block, block.shape[dim] - width, None, axis...]
    pallas_call x0 -> x1, Pallas kernels: none -> 68 us  [per_device(): pl.pallas_call(kernel, out_shape=jax.ShapeDtypeStruct((BLOCKS, BS, BS), f...]
    all_gather x1 -> x0, waiting for transfers between devices: 62.6 us -> none  [per_device(): own_rows = lax.all_gather(density, 'layer', axis=1, tiled=True)]
    gather x16 -> x0, local copies, waits for them, and re-layouts: 46 us -> none  [the longest x8 41.5 us: term_row(): picked = jnp.take(nearby, mine - first + rows, axis=0)]
    dot_general x16 -> x0, matrix products: 26.6 us -> none  [the longest x8 22.2 us: term_row(): jnp.einsum('tij,tujk->tuik', blocks, picked, precision=lax.Precision.HIGH...]
    another operation x1 -> x0, loops' own time: 20.3 us -> none  [per_device(): partial_rows = lax.map(term_row, jnp.arange(rows, dtype=jnp.int32))]
    ppermute x2 -> x0, starting transfers between devices: 13.1 us -> none  [the longest x1 11.1 us: padded(): lax.ppermute(lax.slice_in_dim(block, 0, width, axis=dim), axis, backward)]
  transfers between devices with their start and end apart: 4 -> 0, of which waited for: 3 -> 0; matrix products, arithmetic and copies ran while one was open for 1% -> 0% of each run, Pallas kernels for 0% -> 0%
where the time goes in v1:
time: 71.4 us; the launch traced here: 71.2 us
  Pallas kernels  68 us (95%)
  local copies, waits for them, and re-layouts  3.15 us (4%)
    pallas_call x1, Pallas kernels, per_device(): pl.pallas_call(kernel, out_shape=jax.ShapeDtypeStruct((BLOCKS, BS, BS), f...  68 us
    unnamed x4, local copies, waits for them, and re-layouts  3.15 us

profile of v1, /device:TPU:6, one launch (start us, length us, event | category | flops | bytes accessed | tf_op | source)
XLA Modules:
  0.0 71.2 jit_solution(8341780833329729008)
XLA Ops:
  0.0 0.9 %copy.3.pat_ref = s32[1024,8]{1,0:T(8,128)S(1)} copy(s32[1024,8]{0,1:T(8,128)} %param.2) | data formatting | bytes 65536 | tf_op args[0]
  1.0 0.0 copy-start
  1.0 1.2 %copy-done = f32[8,2,128,128]{3,2,1,0:T(8,128)S(1)} copy-done((f32[8,2,128,128]{3,2,1,0:T(8,128)S(1)}, f32[8,2,128,128]{3,2,1,0:T(8,128)}, u32[]{:S(2)}) %copy-start) | copy-done | bytes 1048600
  2.2 68.0 %shard_map.28 = f32[16,128,128]{2,1,0:T(8,128)S(1)} custom-call(s32[1024,8]{1,0:T(8,128)S(1)} %copy.3.pat_ref, f32[16,128,128]{2,1,0:T(8,128)S(1)} %bitcast.3), custom_call_target="tpu_custom_call" | custom-call | flops 1610612736 | bytes 16777216 | tf_op jit(solution)/shard_map/pallas_call | solution.py:211
  70.2 1.0 %copy.5 = f32[8,2,128,128]{3,2,1,0:T(8,128)} copy(f32[8,2,128,128]{3,2,1,0:T(8,128)S(1)} %bitcast.2) | data formatting | bytes 2097152
Async XLA Ops:
  1.0 1.2 %copy-start = (f32[8,2,128,128]{3,2,1,0:T(8,128)S(1)}, f32[8,2,128,128]{3,2,1,0:T(8,128)}, u32[]{:S(2)}) copy-start(f32[8,2,128,128]{3,2,1,0:T(8,128)} %param.3) | copy-start | bytes 3145732

commit v2 on v1

v2 whole, which is shorter than its diff:
```python
import jax
import jax.numpy as jnp
from jax import lax
from jax.experimental import pallas as pl
from jax.experimental.pallas import tpu as pltpu
from jax.sharding import PartitionSpec as P

MESH = pl.DeviceIdType.MESH
LAYERS, ROWS_AXIS, COLS_AXIS, RUNS = 4, 8, 16, 4
ROWS, SLOTS, QUARTER, BS = 8, 8, 2, 128
BLOCKS = ROWS * QUARTER
GROUP = LAYERS * BLOCKS
TILE = COLS_AXIS * ROWS
REACH = SLOTS - 1
CHUNKS = 4
AHEAD = 4
DIRECT = (1, 2)
CB = BLOCKS // CHUNKS


def kernel(
    pat_ref, den_ref, out_ref,
    near, part, pat, tab_near, tab_part, tab_t, a_hi, a_lo, m_hi, m_lo, acc,
    near_sem, part_sem, send_sem, local_sem, pat_sem,
):
    l, row, col = (lax.axis_index(a) for a in ("layer", "row", "col"))
    core = lax.rem(col, 2)
    g = row * COLS_AXIS + col
    up, dn, opp = lax.rem(l + 1, 4), lax.rem(l + 3, 4), lax.rem(l + 2, 4)
    pg = lax.rem(g + jnp.where(core == 0, 127, 1), 128)
    at_up, at_dn = (up, row, col), (dn, row, col)
    at_mate = (l, row, col + 1 - 2 * core)
    at_part = (l, lax.div(pg, COLS_AXIS), lax.rem(pg, COLS_AXIS))

    def long_way(at_row, at_col):
        at_x = lax.rem(at_row, RUNS)
        return jnp.logical_or(
            jnp.logical_and(at_col == 0, at_x != 0),
            jnp.logical_and(at_col == COLS_AXIS - 1, at_x != RUNS - 1),
        )

    def mate_col(at_col):
        return at_col + 1 - 2 * lax.rem(at_col, 2)

    far = long_way(row, col)
    close = jnp.logical_not(far)
    keep = jnp.logical_not(long_way(row, mate_col(col)))
    give = long_way(at_part[1], mate_col(at_part[2]))

    barrier = pltpu.get_barrier_semaphore()
    for peer in (at_up, at_dn, at_mate, at_part):
        pl.semaphore_signal(barrier, inc=1, device_id=peer, device_id_type=MESH)

    sent = []

    def send(src, dst, sem, peer, when=None):
        n = len(sent)
        copy = pltpu.make_async_remote_copy(
            src_ref=src, dst_ref=dst, send_sem=send_sem.at[n], recv_sem=sem,
            device_id=peer, device_id_type=MESH,
        )
        sent.append((copy, when))
        if when is None:
            copy.start()
        else:
            pl.when(when)(copy.start)

    def piece(ref, base, layer, j):
        return ref.at[pl.ds(base + layer * BLOCKS + j * CB, CB)]

    def own(layer, j):
        return piece(near, 0, layer, j)

    def mate(layer, j):
        return piece(near, GROUP, layer, j)

    def halo(layer, j):
        return piece(part, 0, layer, j)

    def own_sem(layer, j):
        return near_sem.at[layer * CHUNKS + j]

    def mate_sem(layer, j):
        return near_sem.at[LAYERS * CHUNKS + layer * CHUNKS + j]

    def halo_sem(layer, j):
        return part_sem.at[layer * CHUNKS + j]

    def arrived(ref, sem):
        pltpu.make_async_remote_copy(
            src_ref=ref, dst_ref=ref, send_sem=send_sem.at[0], recv_sem=sem,
            device_id=at_mate, device_id_type=MESH,
        ).wait_recv()

    pat_copies = []
    for k in range(3):
        tile = lax.rem(row + ROWS_AXIS - 1 + k, ROWS_AXIS)
        c = pltpu.make_async_copy(
            pat_ref.at[:, pl.ds(pl.multiple_of(tile * TILE, TILE), TILE)], pat.at[pl.ds(k * SLOTS, SLOTS)], pat_sem.at[k]
        )
        c.start()
        pat_copies.append(c)
    mine = pltpu.make_async_copy(den_ref, near.at[pl.ds(l * BLOCKS, BLOCKS)], local_sem)
    mine.start()
    pl.semaphore_wait(barrier, 4)

    def spread(j):
        src = den_ref.at[pl.ds(j * CB, CB)]
        send(src, own(l, j), own_sem(l, j), at_up)
        send(src, own(l, j), own_sem(l, j), at_dn)

    for j in range(CHUNKS):
        src = den_ref.at[pl.ds(j * CB, CB)]
        if j < AHEAD:
            spread(j)
        send(src, halo(l, j), halo_sem(l, j), at_part)
    for j in range(CHUNKS):
        src = den_ref.at[pl.ds(j * CB, CB)]
        send(src, mate(l, j), mate_sem(l, j), at_mate)

    near[2 * GROUP] = jnp.zeros((BS, BS), jnp.float32)
    part[GROUP] = jnp.zeros((BS, BS), jnp.float32)
    for c in pat_copies:
        c.wait()

    def index_row(r, carry):
        here = col * ROWS + r
        wanted = [pat[SLOTS + 2 * l + s, here] for s in range(QUARTER)]
        count = jnp.int32(0)
        far_t = [jnp.int32(0)] * SLOTS
        far_at = [[jnp.int32(GROUP)] * QUARTER for _ in range(SLOTS)]
        for t in range(SLOTS):
            q = jnp.clip(pat[SLOTS + t, here] - TILE * (row - 1), 0, 3 * TILE - 1)
            side, lane = lax.div(q, TILE) * SLOTS, lax.rem(q, TILE)
            grp, qrow = lax.div(q, ROWS) - COLS_AXIS - col, lax.rem(q, ROWS)
            is_own = grp == 0
            is_near = jnp.logical_or(is_own, grp == 1 - 2 * core)
            base = qrow * QUARTER
            at = [jnp.int32(-1)] * QUARTER
            for u in range(SLOTS):
                v = pat[side + u, lane]
                for s in range(QUARTER):
                    at[s] = jnp.where(v == wanted[s], base + (u // 2) * BLOCKS + u % 2, at[s])
            for s in range(QUARTER):
                hit = jnp.logical_and(at[s] >= 0, is_near)
                tab_near[r * 16 + t * 2 + s] = jnp.where(
                    hit, at[s] + jnp.where(is_own, 0, GROUP), 2 * GROUP
                )
            is_far = jnp.logical_not(is_near)
            for j in range(min(t + 1, REACH)):
                here_j = jnp.logical_and(is_far, count == j)
                far_t[j] = jnp.where(here_j, t, far_t[j])
                for s in range(QUARTER):
                    far_at[j][s] = jnp.where(jnp.logical_and(here_j, at[s] >= 0), at[s], far_at[j][s])
            count = count + is_far.astype(jnp.int32)
        for j in range(SLOTS):
            tab_t[r * SLOTS + j] = far_t[j]
            for s in range(QUARTER):
                tab_part[r * 16 + j * 2 + s] = far_at[j][s]
        return carry

    lax.fori_loop(0, ROWS, index_row, 0)

    half = CHUNKS // 2
    for j in range(CHUNKS):
        arrived(own(dn, j), own_sem(dn, j))
        arrived(own(up, j), own_sem(up, j))
        if j + AHEAD < CHUNKS:
            spread(j + AHEAD)
        if j < half:
            send(own(dn, j), own(dn, j), own_sem(dn, j), at_up)
        else:
            send(own(up, j), own(up, j), own_sem(up, j), at_dn)
        if j < half:
            send(own(dn, j), halo(dn, j), halo_sem(dn, j), at_part, close)
        else:
            send(own(up, j), halo(up, j), halo_sem(up, j), at_part, close)
        send(own(dn, j), mate(dn, j), mate_sem(dn, j), at_mate)
        send(own(up, j), mate(up, j), mate_sem(up, j), at_mate)
    for j in range(half):
        send(own(dn, j + half), halo(dn, j + half), halo_sem(dn, j + half), at_part, close)
        send(own(up, j), halo(up, j), halo_sem(up, j), at_part, close)
    for j in range(CHUNKS):
        arrived(halo(l, j), halo_sem(l, j))
        send(halo(l, j), halo(l, j), halo_sem(l, j), at_up, far)
        send(halo(l, j), halo(l, j), halo_sem(l, j), at_dn, far)
    for j in range(half):
        for k in (j, j + half):
            arrived(own(opp, k), own_sem(opp, k))
            send(own(opp, k), mate(opp, k), mate_sem(opp, k), at_mate)
            if k in DIRECT:
                send(own(opp, k), halo(opp, k), halo_sem(opp, k), at_part, give)
    for j in range(half):
        arrived(halo(dn, j), halo_sem(dn, j))
        send(halo(dn, j), halo(dn, j), halo_sem(dn, j), at_up, keep if j in DIRECT else None)
        arrived(halo(up, j + half), halo_sem(up, j + half))
        send(halo(up, j + half), halo(up, j + half), halo_sem(up, j + half), at_dn, keep if j + half in DIRECT else None)
    for j in range(half):
        arrived(halo(dn, j + half), halo_sem(dn, j + half))
        arrived(halo(up, j), halo_sem(up, j))
    mine.wait()
    for layer in range(LAYERS):
        for j in range(CHUNKS):
            arrived(mate(layer, j), mate_sem(layer, j))

    def split(v):
        hi = v.astype(jnp.bfloat16)
        return hi, (v - hi.astype(jnp.float32)).astype(jnp.bfloat16)

    def product(r, ref, tab):
        for t in range(SLOTS):
            for s in range(QUARTER):
                hi, lo = split(ref[tab[r * 16 + t * 2 + s]])
                m_hi[t * BS:(t + 1) * BS, s * BS:(s + 1) * BS] = hi
                m_lo[t * BS:(t + 1) * BS, s * BS:(s + 1) * BS] = lo
        h, low = (jnp.concatenate([a[r * SLOTS + t] for t in range(SLOTS)], axis=1) for a in (a_hi, a_lo))
        w = m_hi[...]
        total = jnp.dot(h, w, preferred_element_type=jnp.float32)
        total += jnp.dot(h, m_lo[...], preferred_element_type=jnp.float32)
        return total + jnp.dot(low, w, preferred_element_type=jnp.float32)

    def near_row(r, carry):
        for t in range(SLOTS):
            hi, lo = split(near[(t // 2) * BLOCKS + r * QUARTER + t % 2])
            a_hi[r * SLOTS + t] = hi
            a_lo[r * SLOTS + t] = lo
        total = product(r, near, tab_near)
        for s in range(QUARTER):
            acc[r * QUARTER + s] = total[:, s * BS:(s + 1) * BS]
        return carry

    lax.fori_loop(0, ROWS, near_row, 0)

    for j in range(CHUNKS):
        arrived(halo(opp, j), halo_sem(opp, j))

    def pair(r, j):
        tiles = [[split(part[tab_part[r * 16 + i * 2 + s]]) for s in range(QUARTER)] for i in (j, j + 1)]
        w_hi, w_lo = (
            jnp.concatenate([jnp.concatenate([b[k] for b in tile], axis=1) for tile in tiles], axis=0) for k in (0, 1)
        )
        h, low = (jnp.concatenate([a[r * SLOTS + tab_t[r * SLOTS + i]] for i in (j, j + 1)], axis=1) for a in (a_hi, a_lo))
        total = jnp.dot(h, w_hi, preferred_element_type=jnp.float32)
        total += jnp.dot(h, w_lo, preferred_element_type=jnp.float32)
        return total + jnp.dot(low, w_hi, preferred_element_type=jnp.float32)

    for i in range(ROWS):
        r = i + core * (ROWS - 1 - 2 * i)
        total = pair(r, 0)
        for j in range(2, min(REACH, ROWS - i), 2):
            total += pair(r, j)
        for s in range(QUARTER):
            out_ref[r * QUARTER + s] = acc[r * QUARTER + s] + total[:, s * BS:(s + 1) * BS]
    for copy, when in sent:
        if when is None:
            copy.wait_send()
        else:
            pl.when(when)(copy.wait_send)


def per_device(pattern, density):
    shape = density.shape
    flat = density.reshape(BLOCKS, BS, BS)
    f32, bf16 = jnp.float32, jnp.bfloat16
    result = pl.pallas_call(
        kernel,
        out_shape=jax.ShapeDtypeStruct((BLOCKS, BS, BS), f32),
        in_specs=[pl.BlockSpec(memory_space=pl.ANY)] * 2,
        out_specs=pl.BlockSpec(memory_space=pltpu.VMEM),
        scratch_shapes=[
            pltpu.VMEM((2 * GROUP + 1, BS, BS), f32),
            pltpu.VMEM((GROUP + 1, BS, BS), f32),
            pltpu.SMEM((3 * SLOTS, TILE), jnp.int32),
            pltpu.SMEM((ROWS * SLOTS * QUARTER,), jnp.int32),
            pltpu.SMEM((ROWS * SLOTS * QUARTER,), jnp.int32),
            pltpu.SMEM((ROWS * SLOTS,), jnp.int32),
            pltpu.VMEM((ROWS * SLOTS, BS, BS), bf16),
            pltpu.VMEM((ROWS * SLOTS, BS, BS), bf16),
            pltpu.VMEM((SLOTS * BS, QUARTER * BS), bf16),
            pltpu.VMEM((SLOTS * BS, QUARTER * BS), bf16),
            pltpu.VMEM((BLOCKS, BS, BS), f32),
            pltpu.SemaphoreType.DMA((2 * LAYERS * CHUNKS,)),
            pltpu.SemaphoreType.DMA((LAYERS * CHUNKS,)),
            pltpu.SemaphoreType.DMA((13 * CHUNKS + len(DIRECT),)),
            pltpu.SemaphoreType.DMA,
            pltpu.SemaphoreType.DMA((3,)),
        ],
        compiler_params=pltpu.CompilerParams(
            collective_id=0, has_side_effects=True, vmem_limit_bytes=40 * 1024 * 1024
        ),
        cost_estimate=pl.CostEstimate(flops=3 * 2**29, bytes_accessed=2**24, transcendentals=0),
    )(pattern.T, flat)
    return result.reshape(shape)


def solution(mesh):
    in_specs = (P(), P(("row", "col"), "layer", None, None))
    out_specs = P(("row", "col"), "layer", None, None)
    return jax.shard_map(
        per_device, mesh=mesh, in_specs=in_specs, out_specs=out_specs, check_vma=False
    )
```

time: 71.4 us -> 66 us (0.924)
  Pallas kernels: 68 us -> 62.3 us
    pallas_call x1, Pallas kernels: 68 us -> 62.3 us  [per_device(): pl.pallas_call(kernel, out_shape=jax.ShapeDtypeStruct((BLOCKS, BS, BS), f...]
    unnamed x4 -> x5, local copies, waits for them, and re-layouts: 3.15 us -> 2.95 us
where the time goes in v2:
time: 66 us; the launch traced here: 65.3 us
  Pallas kernels  62.3 us (94%)
  local copies, waits for them, and re-layouts  2.95 us (4%)
    pallas_call x1, Pallas kernels, per_device(): pl.pallas_call(kernel, out_shape=jax.ShapeDtypeStruct((BLOCKS, BS, BS), f...  62.3 us
    unnamed x5, local copies, waits for them, and re-layouts  2.95 us

profile of v2, /device:TPU:6, one launch (start us, length us, event | category | flops | bytes accessed | tf_op | source)
XLA Modules:
  0.0 65.3 jit_solution(3806823427069897895)
XLA Ops:
  0.0 0.0 copy-start
  0.0 1.2 %copy-done = f32[8,2,128,128]{3,2,1,0:T(8,128)S(1)} copy-done((f32[8,2,128,128]{3,2,1,0:T(8,128)S(1)}, f32[8,2,128,128]{3,2,1,0:T(8,128)}, u32[]{:S(2)}) %copy-start) | copy-done | bytes 1048600
  1.2 0.0 copy-start.1
  1.2 0.8 %copy-done.1 = s32[1024,8]{0,1:T(8,128)S(1)} copy-done((s32[1024,8]{0,1:T(8,128)S(1)}, s32[1024,8]{0,1:T(8,128)}, u32[]{:S(2)}) %copy-start.1) | copy-done | bytes 32792
  2.0 62.3 %shard_map.28 = f32[16,128,128]{2,1,0:T(8,128)S(1)} custom-call(s32[8,1024]{1,0:T(8,128)S(1)} %bitcast.5, f32[16,128,128]{2,1,0:T(8,128)S(1)} %bitcast.4), custom_call_target="tpu_custom_call" | custom-call | flops 1610612736 | bytes 16777216 | tf_op jit(solution)/shard_map/pallas_call | solution.py:265
  64.3 1.0 %copy.4 = f32[8,2,128,128]{3,2,1,0:T(8,128)} copy(f32[8,2,128,128]{3,2,1,0:T(8,128)S(1)} %bitcast.3) | data formatting | bytes 2097152
Async XLA Ops:
  0.0 1.2 %copy-start = (f32[8,2,128,128]{3,2,1,0:T(8,128)S(1)}, f32[8,2,128,128]{3,2,1,0:T(8,128)}, u32[]{:S(2)}) copy-start(f32[8,2,128,128]{3,2,1,0:T(8,128)} %param.3) | copy-start | bytes 3145732
  1.2 0.8 %copy-start.1 = (s32[1024,8]{0,1:T(8,128)S(1)}, s32[1024,8]{0,1:T(8,128)}, u32[]{:S(2)}) copy-start(s32[1024,8]{0,1:T(8,128)} %param.2) | copy-start | bytes 98308

commit v3 on v2

--- a/solution.py
+++ b/solution.py
@@ -14,7 +14,7 @@
 REACH = SLOTS - 1
 CHUNKS = 4
 AHEAD = 4
-DIRECT = (1, 2)
+DIRECT = (0, 2)
 CB = BLOCKS // CHUNKS
 
 
@@ -286,7 +286,7 @@
             pltpu.SemaphoreType.DMA((3,)),
         ],
         compiler_params=pltpu.CompilerParams(
-            collective_id=0, has_side_effects=True, vmem_limit_bytes=40 * 1024 * 1024
+            collective_id=0, has_side_effects=True, vmem_limit_bytes=52 * 1024 * 1024
         ),
         cost_estimate=pl.CostEstimate(flops=3 * 2**29, bytes_accessed=2**24, transcendentals=0),
     )(pattern.T, flat)

time: 66 us -> 64.5 us (0.977)
  local copies, waits for them, and re-layouts: 2.95 us -> 1.73 us
    unnamed x5 -> x3, local copies, waits for them, and re-layouts: 2.95 us -> 1.73 us
where the time goes in v3:
time: 64.5 us; the launch traced here: 64.3 us
  Pallas kernels  62.6 us (97%)
  local copies, waits for them, and re-layouts  1.73 us (3%)
    pallas_call x1, Pallas kernels, per_device(): pl.pallas_call(kernel, out_shape=jax.ShapeDtypeStruct((BLOCKS, BS, BS), f...  62.6 us
    unnamed x3, local copies, waits for them, and re-layouts  1.73 us

profile of v3, /device:TPU:6, one launch (start us, length us, event | category | flops | bytes accessed | tf_op | source)
XLA Modules:
  0.0 64.3 jit_solution(5142248533902574387)
XLA Ops:
  0.0 0.0 copy-start
  0.0 0.8 %copy-done = s32[1024,8]{0,1:T(8,128)S(1)} copy-done((s32[1024,8]{0,1:T(8,128)S(1)}, s32[1024,8]{0,1:T(8,128)}, u32[]{:S(2)}) %copy-start) | copy-done | bytes 32792
  0.8 62.6 %shard_map.28 = f32[16,128,128]{2,1,0:T(8,128)S(1)} custom-call(s32[8,1024]{1,0:T(8,128)S(1)} %bitcast.4, f32[16,128,128]{2,1,0:T(8,128)} %bitcast.5), custom_call_target="tpu_custom_call" | custom-call | flops 1610612736 | bytes 16777216 | tf_op jit(solution)/shard_map/pallas_call | solution.py:265
  63.3 1.0 %copy.4 = f32[8,2,128,128]{3,2,1,0:T(8,128)} copy(f32[8,2,128,128]{3,2,1,0:T(8,128)S(1)} %bitcast.3) | data formatting | bytes 2097152
Async XLA Ops:
  0.0 0.8 %copy-start = (s32[1024,8]{0,1:T(8,128)S(1)}, s32[1024,8]{0,1:T(8,128)}, u32[]{:S(2)}) copy-start(s32[1024,8]{0,1:T(8,128)} %param.2) | copy-start | bytes 98308

commit v4 on v3

--- a/solution.py
+++ b/solution.py
@@ -13,7 +13,6 @@
 TILE = COLS_AXIS * ROWS
 REACH = SLOTS - 1
 CHUNKS = 4
-AHEAD = 4
 DIRECT = (0, 2)
 CB = BLOCKS // CHUNKS
 
@@ -104,16 +103,17 @@
     mine.start()
     pl.semaphore_wait(barrier, 4)
 
-    def spread(j):
+    half = CHUNKS // 2
+
+    def later(j):
+        return (j + half) % CHUNKS
+
+    for j in range(CHUNKS):
         src = den_ref.at[pl.ds(j * CB, CB)]
+        other = den_ref.at[pl.ds(later(j) * CB, CB)]
+        send(src, halo(l, j), halo_sem(l, j), at_part)
         send(src, own(l, j), own_sem(l, j), at_up)
-        send(src, own(l, j), own_sem(l, j), at_dn)
-
-    for j in range(CHUNKS):
-        src = den_ref.at[pl.ds(j * CB, CB)]
-        if j < AHEAD:
-            spread(j)
-        send(src, halo(l, j), halo_sem(l, j), at_part)
+        send(other, own(l, later(j)), own_sem(l, later(j)), at_dn)
     for j in range(CHUNKS):
         src = den_ref.at[pl.ds(j * CB, CB)]
         send(src, mate(l, j), mate_sem(l, j), at_mate)
@@ -161,25 +161,17 @@
 
     lax.fori_loop(0, ROWS, index_row, 0)
 
-    half = CHUNKS // 2
-    for j in range(CHUNKS):
+    for j in range(CHUNKS):
+        k = later(j)
         arrived(own(dn, j), own_sem(dn, j))
-        arrived(own(up, j), own_sem(up, j))
-        if j + AHEAD < CHUNKS:
-            spread(j + AHEAD)
+        arrived(own(up, k), own_sem(up, k))
+        send(own(dn, j), halo(dn, j), halo_sem(dn, j), at_part, close)
+        send(own(up, k), halo(up, k), halo_sem(up, k), at_part, close)
         if j < half:
             send(own(dn, j), own(dn, j), own_sem(dn, j), at_up)
-        else:
-            send(own(up, j), own(up, j), own_sem(up, j), at_dn)
-        if j < half:
-            send(own(dn, j), halo(dn, j), halo_sem(dn, j), at_part, close)
-        else:
-            send(own(up, j), halo(up, j), halo_sem(up, j), at_part, close)
+            send(own(up, k), own(up, k), own_sem(up, k), at_dn)
         send(own(dn, j), mate(dn, j), mate_sem(dn, j), at_mate)
-        send(own(up, j), mate(up, j), mate_sem(up, j), at_mate)
-    for j in range(half):
-        send(own(dn, j + half), halo(dn, j + half), halo_sem(dn, j + half), at_part, close)
-        send(own(up, j), halo(up, j), halo_sem(up, j), at_part, close)
+        send(own(up, k), mate(up, k), mate_sem(up, k), at_mate)
     for j in range(CHUNKS):
         arrived(halo(l, j), halo_sem(l, j))
         send(halo(l, j), halo(l, j), halo_sem(l, j), at_up, far)

time: 64.5 us -> 64.5 us (level)
  no operation moved by 1% of the time
where the time goes in v4:
time: 64.5 us; the launch traced here: 64.3 us
  Pallas kernels  62.6 us (97%)
  local copies, waits for them, and re-layouts  1.73 us (3%)
    pallas_call x1, Pallas kernels, per_device(): pl.pallas_call(kernel, out_shape=jax.ShapeDtypeStruct((BLOCKS, BS, BS), f...  62.6 us
    unnamed x3, local copies, waits for them, and re-layouts  1.73 us

profile of v4, /device:TPU:6, one launch (start us, length us, event | category | flops | bytes accessed | tf_op | source)
XLA Modules:
  0.0 64.3 jit_solution(1555056325451529398)
XLA Ops:
  0.0 0.0 copy-start
  0.0 0.8 %copy-done = s32[1024,8]{0,1:T(8,128)S(1)} copy-done((s32[1024,8]{0,1:T(8,128)S(1)}, s32[1024,8]{0,1:T(8,128)}, u32[]{:S(2)}) %copy-start) | copy-done | bytes 32792
  0.8 62.6 %shard_map.28 = f32[16,128,128]{2,1,0:T(8,128)S(1)} custom-call(s32[8,1024]{1,0:T(8,128)S(1)} %bitcast.4, f32[16,128,128]{2,1,0:T(8,128)} %bitcast.5), custom_call_target="tpu_custom_call" | custom-call | flops 1610612736 | bytes 16777216 | tf_op jit(solution)/shard_map/pallas_call | solution.py:257
  63.4 1.0 %copy.4 = f32[8,2,128,128]{3,2,1,0:T(8,128)} copy(f32[8,2,128,128]{3,2,1,0:T(8,128)S(1)} %bitcast.3) | data formatting | bytes 2097152
Async XLA Ops:
  0.0 0.8 %copy-start = (s32[1024,8]{0,1:T(8,128)S(1)}, s32[1024,8]{0,1:T(8,128)}, u32[]{:S(2)}) copy-start(s32[1024,8]{0,1:T(8,128)} %param.2) | copy-start | bytes 98308

commit v5 on v3

--- a/solution.py
+++ b/solution.py
@@ -14,7 +14,7 @@
 REACH = SLOTS - 1
 CHUNKS = 4
 AHEAD = 4
-DIRECT = (0, 2)
+DIRECT = (0, 2, 3)
 CB = BLOCKS // CHUNKS
 
 

time: 64.5 us -> 65.1 us (level)
  no operation moved by 1% of the time
where the time goes in v5:
time: 65.1 us; the launch traced here: 64.3 us
  Pallas kernels  62.6 us (96%)
  local copies, waits for them, and re-layouts  1.73 us (3%)
    pallas_call x1, Pallas kernels, per_device(): pl.pallas_call(kernel, out_shape=jax.ShapeDtypeStruct((BLOCKS, BS, BS), f...  62.6 us
    unnamed x3, local copies, waits for them, and re-layouts  1.73 us

profile of v5, /device:TPU:6, one launch (start us, length us, event | category | flops | bytes accessed | tf_op | source)
XLA Modules:
  0.0 64.3 jit_solution(16599923858213917253)
XLA Ops:
  0.0 0.0 copy-start
  0.0 0.8 %copy-done = s32[1024,8]{0,1:T(8,128)S(1)} copy-done((s32[1024,8]{0,1:T(8,128)S(1)}, s32[1024,8]{0,1:T(8,128)}, u32[]{:S(2)}) %copy-start) | copy-done | bytes 32792
  0.8 62.6 %shard_map.28 = f32[16,128,128]{2,1,0:T(8,128)S(1)} custom-call(s32[8,1024]{1,0:T(8,128)S(1)} %bitcast.4, f32[16,128,128]{2,1,0:T(8,128)} %bitcast.5), custom_call_target="tpu_custom_call" | custom-call | flops 1610612736 | bytes 16777216 | tf_op jit(solution)/shard_map/pallas_call | solution.py:265
  63.3 1.0 %copy.4 = f32[8,2,128,128]{3,2,1,0:T(8,128)} copy(f32[8,2,128,128]{3,2,1,0:T(8,128)S(1)} %bitcast.3) | data formatting | bytes 2097152
Async XLA Ops:
  0.0 0.8 %copy-start = (s32[1024,8]{0,1:T(8,128)S(1)}, s32[1024,8]{0,1:T(8,128)}, u32[]{:S(2)}) copy-start(s32[1024,8]{0,1:T(8,128)} %param.2) | copy-start | bytes 98308
